TPU v7x, 32 devices: a whole 2x2x4 slice. The times are simulated.
32 devices in a mesh: dp: 8 (over z, y), head: 4 (over x, core).
Axes of the slice: x: 2, y: 2, z: 4, core: 2. Of those that a mesh axis runs over, the one named last changes fastest.
Arguments:
- tokens: bfloat16 [18432, 768], P(('dp', 'head')), may hold values from -6 to 6
- w_qkv: bfloat16 [3, 768, 768], P(None, None, 'head'), may hold values from -0.21875 to 0.21875
- b_qv: bfloat16 [2, 768], P(None, 'head'), may hold values from -1.796875 to 1.796875
- w_out: bfloat16 [768, 768], P('head'), may hold values from -0.875 to 0.875
- b_out: bfloat16 [768], replicated, may hold values from -1.796875 to 1.796875
- gain_one: bfloat16 [768], replicated, may hold values from 0.5 to 1.5
- shift_one: bfloat16 [768], replicated, may hold values from -1.796875 to 1.796875
- w_in: bfloat16 [768, 3072], replicated, may hold values from -0.21875 to 0.21875
- b_in: bfloat16 [3072], replicated, may hold values from -1.796875 to 1.796875
- w_down: bfloat16 [3072, 768], replicated, may hold values from -0.109375 to 0.109375
- b_down: bfloat16 [768], replicated, may hold values from -1.796875 to 1.796875
- gain_two: bfloat16 [768], replicated, may hold values from 0.5 to 1.5
- shift_two: bfloat16 [768], replicated, may hold values from -1.796875 to 1.796875
- w_term: bfloat16 [768], replicated, may hold values from -0.21875 to 0.21875
- b_term: bfloat16 [1], replicated, may hold values from -3 to 3
- pass_len: int32 [32], P('dp'), may hold values from 40 to 512, as said below
- query_len: int32 [64], P('dp'), may hold values from 8 to 32, as said below
- grad_out: bfloat16 [18432, 768], P(('dp', 'head')), may hold values from -6 to 6
- grad_term: float32 [18432], P(('dp', 'head')), may hold values from -6 to 6
Outputs:
- out: bfloat16 [18432, 768], P(('dp', 'head'))
- term: float32 [18432], P(('dp', 'head'))
- grad_tokens: bfloat16 [18432, 768], P(('dp', 'head'))
- grad_w_qkv: float32 [3, 768, 768], P(None, None, 'head')
- grad_b_qv: float32 [2, 768], P(None, 'head')
- grad_w_out: float32 [768, 768], P('head')
- grad_b_out: float32 [768], replicated
- grad_gain_one: float32 [768], replicated
- grad_shift_one: float32 [768], replicated
- grad_w_in: float32 [768, 3072], P(None, ('dp', 'head'))
- grad_b_in: float32 [3072], replicated
- grad_w_down: float32 [3072, 768], P(('dp', 'head'))
- grad_b_down: float32 [768], replicated
- grad_gain_two: float32 [768], replicated
- grad_shift_two: float32 [768], replicated
- grad_w_term: float32 [768], replicated
- grad_b_term: float32 [1], replicated
Inputs may be any that keep to these rules, and one draw needn't show every extreme that they name: `pass_len`: among the passages of each index of dp, one drawn from the seed has length exactly 512. `query_len`: among the queries of each index of dp, one drawn from the seed has length exactly 32.
All inputs are finite; a program needn't handle non-finite values.
Results may differ from a plain program's by a relative error of at most 0.014.
The roundings to bfloat16 on the way count: a program that leaves them out, or rounds other values in their place, can miss the bound.
Values may be sent and summed in bfloat16 or wider, within the bound.
No kernel may reach another device: no remote copies, remote signals or barrier semaphores. Data moves between devices by JAX's collectives and lax.ppermute only.
A program may use at most 192 MiB of HBM per device.

v0:
```python
import math

import jax
import jax.numpy as jnp
from jax import lax
from jax.sharding import PartitionSpec as P

HEAD_DIM = 64
PLEN = 512
QLEN = 32


def split_heads(block, number, length):
    return block.reshape(number, length, -1, HEAD_DIM)


def scores_of(query, keys, lengths):
    scores = jnp.einsum("sqhd,skhd->shqk", query, keys, preferred_element_type=jnp.float32) * (
        1.0 / math.sqrt(HEAD_DIM)
    )
    valid = jnp.arange(keys.shape[1], dtype=jnp.int32)[None, :] < lengths[:, None]
    return jnp.where(valid[:, None, None, :], scores, -1000000000.0)


def attend_forward(query, keys, values, lengths):
    scores = scores_of(query, keys, lengths)
    row_max = jnp.max(scores, -1, keepdims=True)
    exponent = jnp.exp(scores - row_max)
    total = jnp.sum(exponent, -1, keepdims=True)
    shares = (exponent / total).astype(jnp.bfloat16)
    mixed = jnp.einsum(
        "shqk,skhd->sqhd", shares, values, preferred_element_type=jnp.float32
    ).astype(jnp.bfloat16)
    return (mixed, row_max + jnp.log(total))


def attend_backward(query, keys, values, lengths, log_total, grad_mixed):
    scores = scores_of(query, keys, lengths)
    shares = jnp.exp(scores - log_total)
    grad_shares = jnp.einsum(
        "sqhd,skhd->shqk", grad_mixed, values, preferred_element_type=jnp.float32
    )
    grad_values = jnp.einsum(
        "shqk,sqhd->skhd",
        shares.astype(jnp.bfloat16),
        grad_mixed,
        preferred_element_type=jnp.float32,
    )
    inner_sum = jnp.sum(shares * grad_shares, -1, keepdims=True)
    grad_scores = (shares * (grad_shares - inner_sum)).astype(jnp.bfloat16)
    scale = 1.0 / math.sqrt(HEAD_DIM)
    grad_query = (
        jnp.einsum("shqk,skhd->sqhd", grad_scores, keys, preferred_element_type=jnp.float32) * scale
    )
    grad_keys = (
        jnp.einsum("shqk,sqhd->skhd", grad_scores, query, preferred_element_type=jnp.float32)
        * scale
    )
    return (grad_query, grad_keys, grad_values)


def normalize(hidden, gain, shift):
    center = hidden - jnp.mean(hidden, -1, keepdims=True)
    inverse = lax.rsqrt(jnp.mean(center * center, -1, keepdims=True) + 1e-06)
    unit = center * inverse
    return (unit * gain + shift, unit, inverse)


def normalize_back(grad, unit, inverse, gain):
    grad_unit = grad * gain
    return inverse * (
        grad_unit
        - jnp.mean(grad_unit, -1, keepdims=True)
        - unit * jnp.mean(grad_unit * unit, -1, keepdims=True)
    )


def shards(
    tokens,
    w_qkv,
    b_qv,
    w_out,
    b_out,
    gain_one,
    shift_one,
    w_in,
    b_in,
    w_down,
    b_down,
    gain_two,
    shift_two,
    w_term,
    b_term,
    pass_len,
    query_len,
    grad_out,
    grad_term,
):
    local_width = w_qkv.shape[2]
    passages = pass_len.shape[0]
    queries = query_len.shape[0]
    split = passages * PLEN
    qkv_bias = jnp.stack([b_qv[0], jnp.zeros_like(b_qv[0]), b_qv[1]]).astype(jnp.float32)
    gathered = lax.all_gather(tokens, "head", axis=0, tiled=True)
    stacked = (
        jnp.einsum("td,kde->kte", gathered, w_qkv, preferred_element_type=jnp.float32)
        + qkv_bias[:, None, :]
    ).astype(jnp.bfloat16)
    long_qkv = [split_heads(stacked[member, :split], passages, PLEN) for member in range(3)]
    short_qkv = [split_heads(stacked[member, split:], queries, QLEN) for member in range(3)]
    long_mixed, long_total = attend_forward(long_qkv[0], long_qkv[1], long_qkv[2], pass_len)
    short_mixed, short_total = attend_forward(short_qkv[0], short_qkv[1], short_qkv[2], query_len)
    context = jnp.concatenate(
        [long_mixed.reshape(split, local_width), short_mixed.reshape(queries * QLEN, local_width)],
        0,
    )
    context_local = lax.all_to_all(context, "head", split_axis=0, concat_axis=1, tiled=True)
    full_out = lax.all_gather(w_out, "head", axis=0, tiled=True)
    attention = jnp.dot(context_local, full_out, preferred_element_type=jnp.float32)
    gain_first = gain_one.astype(jnp.float32)
    gain_second = gain_two.astype(jnp.float32)
    residual = tokens.astype(jnp.float32) + (attention + b_out.astype(jnp.float32))
    first, first_unit, first_inverse = normalize(
        residual, gain_first, shift_one.astype(jnp.float32)
    )
    first_low = first.astype(jnp.bfloat16)
    inner = jnp.dot(first_low, w_in, preferred_element_type=jnp.float32) + b_in.astype(jnp.float32)
    active, gelu_back = jax.vjp(jax.nn.gelu, inner)
    active_low = active.astype(jnp.bfloat16)
    second_in = (
        first
        + jnp.dot(active_low, w_down, preferred_element_type=jnp.float32)
        + b_down.astype(jnp.float32)
    )
    second, second_unit, second_inverse = normalize(
        second_in, gain_second, shift_two.astype(jnp.float32)
    )
    term_weight = w_term.astype(jnp.float32)
    logit = (
        jnp.dot(
            second, term_weight, precision=lax.Precision.HIGHEST, preferred_element_type=jnp.float32
        )
        + b_term.astype(jnp.float32)[0]
    )
    term = jax.nn.softplus(logit)
    grad_logit = grad_term * jax.nn.sigmoid(logit)
    grad_w_term = jnp.dot(
        grad_logit, second, precision=lax.Precision.HIGHEST, preferred_element_type=jnp.float32
    )
    grad_b_term = jnp.sum(grad_logit)[None]
    grad_second = grad_out.astype(jnp.float32) + grad_logit[:, None] * term_weight[None, :]
    grad_gain_two = jnp.sum(grad_second * second_unit, 0)
    grad_shift_two = jnp.sum(grad_second, 0)
    grad_middle = normalize_back(grad_second, second_unit, second_inverse, gain_second)
    grad_b_down = jnp.sum(grad_middle, 0)
    grad_middle_low = grad_middle.astype(jnp.bfloat16)
    grad_w_down = jnp.einsum(
        "tf,td->fd", active_low, grad_middle_low, preferred_element_type=jnp.float32
    )
    grad_active = jnp.einsum(
        "td,fd->tf", grad_middle_low, w_down, preferred_element_type=jnp.float32
    )
    grad_inner = gelu_back(grad_active)[0]
    grad_b_in = jnp.sum(grad_inner, 0)
    grad_inner_low = grad_inner.astype(jnp.bfloat16)
    grad_w_in = jnp.einsum(
        "td,tf->df", first_low, grad_inner_low, preferred_element_type=jnp.float32
    )
    grad_first = grad_middle + jnp.einsum(
        "tf,df->td", grad_inner_low, w_in, preferred_element_type=jnp.float32
    )
    grad_gain_one = jnp.sum(grad_first * first_unit, 0)
    grad_shift_one = jnp.sum(grad_first, 0)
    grad_residual = normalize_back(grad_first, first_unit, first_inverse, gain_first)
    grad_b_out = jnp.sum(grad_residual, 0)
    grad_attention = grad_residual.astype(jnp.bfloat16)
    grad_full_out = jnp.einsum(
        "te,td->ed", context_local, grad_attention, preferred_element_type=jnp.float32
    )
    grad_context_local = jnp.einsum(
        "td,ed->te", grad_attention, full_out, preferred_element_type=jnp.float32
    ).astype(jnp.bfloat16)
    grad_context = lax.all_to_all(
        grad_context_local, "head", split_axis=1, concat_axis=0, tiled=True
    )
    grad_w_out = lax.psum_scatter(grad_full_out, "head", scatter_dimension=0, tiled=True)
    long_grads = attend_backward(
        long_qkv[0],
        long_qkv[1],
        long_qkv[2],
        pass_len,
        long_total,
        split_heads(grad_context[:split], passages, PLEN),
    )
    short_grads = attend_backward(
        short_qkv[0],
        short_qkv[1],
        short_qkv[2],
        query_len,
        short_total,
        split_heads(grad_context[split:], queries, QLEN),
    )
    grad_stacked = jnp.stack(
        [
            jnp.concatenate(
                [
                    long_grads[member].reshape(split, local_width),
                    short_grads[member].reshape(queries * QLEN, local_width),
                ],
                0,
            )
            for member in range(3)
        ]
    ).astype(jnp.bfloat16)
    grad_b_qv = jnp.stack(
        [
            jnp.sum(grad_stacked[0], 0, dtype=jnp.float32),
            jnp.sum(grad_stacked[2], 0, dtype=jnp.float32),
        ]
    )
    grad_w_qkv = jnp.einsum(
        "td,kte->kde", gathered, grad_stacked, preferred_element_type=jnp.float32
    )
    grad_token_qkv = lax.all_to_all(grad_stacked, "head", split_axis=1, concat_axis=2, tiled=True)
    full_qkv = lax.all_gather(w_qkv, "head", axis=2, tiled=True)
    grad_rows = jnp.einsum(
        "kte,kde->td", grad_token_qkv, full_qkv, preferred_element_type=jnp.float32
    )
    grad_tokens = (grad_residual + grad_rows).astype(jnp.bfloat16)
    vectors = lax.psum(
        (
            grad_b_out,
            grad_gain_one,
            grad_shift_one,
            grad_b_in,
            grad_b_down,
            grad_gain_two,
            grad_shift_two,
            grad_w_term,
            grad_b_term,
        ),
        "head",
    )
    summed = lax.psum(
        (
            grad_w_qkv,
            grad_b_qv,
            grad_w_out,
            vectors[0],
            vectors[1],
            vectors[2],
            vectors[3],
            vectors[4],
            vectors[5],
            vectors[6],
            vectors[7],
            vectors[8],
        ),
        "dp",
    )
    grad_w_in, grad_w_down = (
        lax.psum_scatter(grad_w_in, ("dp", "head"), scatter_dimension=1, tiled=True),
        lax.psum_scatter(grad_w_down, ("dp", "head"), scatter_dimension=0, tiled=True),
    )
    return (
        second.astype(jnp.bfloat16),
        term,
        grad_tokens,
        summed[0],
        summed[1],
        summed[2],
        summed[3],
        summed[4],
        summed[5],
        grad_w_in,
        summed[6],
        grad_w_down,
        summed[7],
        summed[8],
        summed[9],
        summed[10],
        summed[11],
    )


def solution(mesh):
    placed = (
        P(("dp", "head"), None),
        P(None, None, "head"),
        P(None, "head"),
        P("head", None),
        P(),
        P(),
        P(),
        P(),
        P(),
        P(),
        P(),
        P(),
        P(),
        P(),
        P(),
        P("dp"),
        P("dp"),
        P(("dp", "head"), None),
        P(("dp", "head")),
    )
    return jax.shard_map(
        shards,
        mesh=mesh,
        in_specs=placed,
        out_specs=(
            P(("dp", "head"), None),
            P(("dp", "head")),
            P(("dp", "head"), None),
            P(None, None, "head"),
            P(None, "head"),
            P("head", None),
            P(),
            P(),
            P(),
            P(None, ("dp", "head")),
            P(),
            P(("dp", "head"), None),
            P(),
            P(),
            P(),
            P(),
            P(),
        ),
        check_vma=False,
    )
```

profile of v0, /device:TPU:1, one launch (start us, length us, event | category | flops | bytes accessed | tf_op | source)
XLA Modules:
  0.0 595.7 jit_solution(1067578215736832728)
XLA Ops:
  11.0 31.8 %all-gather.4.cloned.1.call-done = bf16[2304,768]{1,0:T(8,128)(2,1)} async-done(((bf16[576,768]{1,0:T(8,128)(2,1)}), bf16[2304,768]{1,0:T(8,128)(2,1)}) %all-gather.4.cloned.1.call-update) | async-done | bytes 3538960 | tf_op jit(solution)/shard_map/all_gather | solution.py:104
  42.9 4.5 fusion.13
  50.6 3.1 fusion.12
  53.8 3.5 fusion
  59.2 3.8 fusion.44
  69.8 3.7 all-to-all-start
  74.7 11.8 %all-to-all-done = bf16[4,576,192]{1,2,0:T(8,128)(2,1)S(1)} async-done(((bf16[4,576,192]{1,2,0:T(8,128)(2,1)}), bf16[4,576,192]{1,2,0:T(8,128)(2,1)S(1)}, u32[]{:S(2)}, u32[]{:S(2)}) %all-to-all-start) | async-done | bytes 884768 | tf_op jit(solution)/shard_map/all_to_all | solution.py:117
  86.5 2.6 fusion.97
  89.5 5.8 fusion.88
  95.3 4.7 fusion.98
  104.6 2.4 fusion.91
  107.0 8.0 %fusion.99 = (f32[3072]{0:T(1024)}, bf16[576,3072]{1,0:T(8,128)(2,1)S(1)}) fusion(f32[576,3072]{1,0:T(8,128)S(1)} %fusion.88, f32[3072]{0:T(1024)S(1)} %convert_element_type.121, bf16[3072,768]{1,0:T(8,128)(2,1)S(1)} %bitcast.159, f32[576,768]{1,0:T(8,128)S(1)} %get-tuple-element.49), kind=kOutput, calls=%fused_computation.148 | convolution fusion | flops 2757276672 | bytes 17129472 | tf_op jit(solution)/shard_map/td,fd->tf/dot_general | solution.py:160
  115.1 4.0 multiply_reduce_fusion.2
  120.2 2.5 fusion.68
  122.7 2.2 convolution_convert_fusion
  126.3 4.4 all-to-all-start.1
  131.9 12.2 %all-to-all-done.1 = bf16[576,4,192]{0,2,1:T(8,128)(2,1)S(1)} async-done(((bf16[576,4,192]{0,2,1:T(8,128)(2,1)}), bf16[576,4,192]{0,2,1:T(8,128)(2,1)S(1)}, u32[]{:S(2)}, u32[]{:S(2)}) %all-to-all-start.1) | async-done | bytes 884768 | tf_op jit(solution)/shard_map/all_to_all | solution.py:183
  147.4 6.6 %fusion.39 = bf16[4,512,3,64]{1,3,2,0:T(8,128)(2,1)S(1)} fusion(f32[4,3,512]{2,1,0:T(4,128)} %log_add_fusion, f32[4,3,512,512]{2,3,1,0:T(8,128)} %copy-done, pred[4,512]{1,0:T(4,128)(4,1)} %copy-done.32, bf16[4,512,3,64]{1,0,3,2:T(4,128)(2,1)S(1)} %reshape.204), kind=kOutput, calls=%fused_computation.65 | convolution fusion | flops 415629312 | bytes 14182400 | tf_op jit(solution)/shard_map/shqk,sqhd->skhd/dot_general | solution.py:43
  159.1 8.4 %multiply_reduce_fusion = (f32[4,3,512]{2,1,0:T(4,128)S(1)}, f32[4,3,512,512]{2,3,1,0:T(8,128)S(1)}) fusion(f32[4,3,512]{2,1,0:T(4,128)S(1)} %copy-done.31, f32[4,3,512,512]{2,3,1,0:T(8,128)} %copy-done, pred[4,512]{1,0:T(4,128)(4,1)S(1)} %copy-done.33, bf16[4,512,3,64]{1,0,3,2:T(4,128)(2,1)} %copy-done.18, bf16[4,512,3,64]{1,0,3,2:T(4,128)(2,1)} %copy-done.19), kind=kOutput, calls=%fused_computation.1 | convolution fusion | flops 418375680 | bytes 26789888 | tf_op jit(solution)/shard_map/sqhd,skhd->shqk/dot_general | solution.py:40
  167.7 4.5 multiply_convert_fusion
  180.6 3.5 fusion.26
  184.2 11.9 %fusion.71 = f32[3072,768]{1,0:T(8,128)} fusion(f32[576,768]{1,0:T(8,128)S(1)} %copy-done.22, f32[576,3072]{1,0:T(8,128)} %copy-done.69, f32[3072]{0:T(1024)S(1)} %copy-done.56), kind=kOutput, calls=%fused_computation.104 | convolution fusion | flops 2736046080 | bytes 18296832 | tf_op jit(solution)/shard_map/tf,td->fd/dot_general | solution.py:157
  197.6 10.2 %fusion.18 = f32[768,3072]{0,1:T(8,128)} fusion(bf16[576,3072]{1,0:T(8,128)(2,1)} %copy-done.70, f32[576,768]{1,0:T(8,128)S(1)} %copy-done.11, f32[768]{0:T(1024)S(1)} %copy-done.61, f32[768]{0:T(1024)S(1)} %copy-done.52, f32[576]{0:T(1024)S(1)} %copy-done.54, f32[576]{0:T(1024)S(1)} %copy-done.50), kind=kOutput, calls=%fused_computation.35 | convolution fusion | flops 2720120832 | bytes 14756352 | tf_op jit(solution)/shard_map/td,tf->df/dot_general | solution.py:166
  209.8 5.4 copy.139
  215.2 7.4 %all-to-all-start.2 = ((bf16[3,2304,192]{2,0,1:T(4,128)(2,1)}), bf16[3,2304,192]{2,0,1:T(4,128)(2,1)}, u32[]{:S(2)}, u32[]{:S(2)}) async-start(bf16[3,2304,192]{2,0,1:T(4,128)(2,1)} %copy.139), calls=%async_computation.2 | async-start | bytes 9437184 | tf_op jit(solution)/shard_map/all_to_all | solution.py:224
  225.3 57.7 %all-reduce.2 = (f32[768]{0:T(1024)S(1)}, f32[768]{0:T(1024)S(1)}, f32[768]{0:T(1024)S(1)}, f32[3072]{0:T(1024)S(1)}, f32[768]{0:T(1024)S(1)}, /*index=5*/f32[76...) all-reduce(f32[768]{0:T(1024)} %get-tuple-element.50, ...), channel_id=1, replica_groups=mesh['dp'=8,'head'=4] {'head'}, use_global_device_ids=true, to_apply=%region_21.22 | all-reduce | flops 8449 | bytes 67592 | tf_op jit(solution)/shard_map/psum | solution.py:230
  283.4 32.2 %all-reduce = (f32[2,192]{1,0:T(2,128)}, f32[768]{0:T(1024)}, f32[768]{0:T(1024)}, f32[768]{0:T(1024)}, f32[3072]{0:T(1024)}, /*index=5*/f32[768]{0:T(1024)}, f3...) all-reduce(f32[2,192]{1,0:T(2,128)S(1)} %pad_maximum_fusion.2, ...), channel_id=1, replica_groups=mesh['dp'=8,'head'=4] {'dp'}, use_global_device_ids=true, to_apply=%region_17.18 | all-reduce | flops 8833 | bytes 70664 | tf_op jit(solution)/shard_map/psum | solution.py:244
  315.7 8.6 %copy.140 = bf16[3,4,576,192]{2,3,1,0:T(8,128)(2,1)} copy(bf16[3,4,576,192]{3,0,2,1:T(4,128)(2,1)} %bitcast.18) | data formatting | bytes 5308416 | tf_op jit(solution)/shard_map/all_to_all | solution.py:224
  324.3 6.4 %fusion.17 = bf16[576,768]{1,0:T(8,128)(2,1)} fusion(f32[576,768]{1,0:T(8,128)S(1)} %copy-done.4, bf16[3,576,768]{1,2,0:T(8,128)(2,1)} %bitcast.142, bf16[3,768,768]{1,2,0:T(8,128)(2,1)} %all-gather.8.cloned.1.call-done), kind=kOutput, calls=%fused_computation.28 | convolution fusion | flops 2039316480 | bytes 8847360 | tf_op jit(solution)/shard_map/kte,kde->td/dot_general | solution.py:226
  330.7 112.0 %reduce-scatter.8.cloned.1.call-done = f32[96,768]{1,0:T(8,128)} async-done(((f32[3072,768]{1,0:T(8,128)}), f32[96,768]{1,0:T(8,128)}) %reduce-scatter.8.cloned.1.call-update) | async-done | bytes 294928 | tf_op jit(solution)/shard_map/reduce_scatter | solution.py:263
  442.7 142.1 %reduce-scatter.6.cloned.1.call-done = f32[768,96]{0,1:T(8,128)} async-done(((f32[768,3072]{0,1:T(8,128)}), f32[768,96]{0,1:T(8,128)}) %reduce-scatter.6.cloned.1.call-update) | async-done | bytes 294928 | tf_op jit(solution)/shard_map/reduce_scatter | solution.py:262
  584.8 2.8 copy.196
  (265 shorter events, 48.6 us)
Async XLA Ops:
  7.2 35.7 %all-gather.4.cloned.1.call-start = ((), (), s32[]{:S(2)}) async-start(), calls=%async_computation.6 | async-start | bytes 4423680 | tf_op jit(solution)/shard_map/all_gather | solution.py:104
  7.9 66.8 %all-gather.6.cloned.1.call-start = ((), (), s32[]{:S(2)}) async-start(), calls=%async_computation.7 | async-start | bytes 1474560 | tf_op jit(solution)/shard_map/all_gather | solution.py:118
  10.1 47.2 %copy-start.32 = (pred[4,512]{1,0:T(4,128)(4,1)}, pred[4,512]{1,0:T(4,128)(4,1)S(1)}, u32[]{:S(2)}) copy-start(pred[4,512]{1,0:T(4,128)(4,1)S(1)} %iota_compare_fusion) | copy-start | bytes 6148
  69.8 16.6 %all-to-all-start = ((bf16[4,576,192]{1,2,0:T(8,128)(2,1)}), bf16[4,576,192]{1,2,0:T(8,128)(2,1)S(1)}, u32[]{:S(2)}, u32[]{:S(2)}) async-start(bf16[4,576,192]{1,2,0:T(8,128)(2,1)} %copy.112), calls=%async_computation | async-start | bytes 1966080 | tf_op jit(solution)/shard_map/all_to_all | solution.py:117
  73.6 110.5 %reduce-scatter.4.cloned.1.call-start = ((), (), s32[]{:S(2)}) async-start(), calls=%async_computation.9 | async-start | bytes 2949120 | tf_op jit(solution)/shard_map/reduce_scatter | solution.py:186
  74.5 44.5 %copy-start.51 = (f32[768]{0:T(1024)}, f32[768]{0:T(1024)S(1)}, u32[]{:S(2)}) copy-start(f32[768]{0:T(1024)S(1)} %convert_element_type.118) | copy-start | bytes 9220
  74.6 30.0 %copy-start.40 = (f32[768]{0:T(1024)}, f32[768]{0:T(1024)S(1)}, u32[]{:S(2)}) copy-start(f32[768]{0:T(1024)S(1)} %convert_element_type.124) | copy-start | bytes 9220
  74.6 20.7 %copy-start.60 = (f32[768]{0:T(1024)}, f32[768]{0:T(1024)S(1)}, u32[]{:S(2)}) copy-start(f32[768]{0:T(1024)S(1)} %convert_element_type.119) | copy-start | bytes 9220
  74.6 30.0 %copy-start.44 = (f32[768]{0:T(1024)}, f32[768]{0:T(1024)S(1)}, u32[]{:S(2)}) copy-start(f32[768]{0:T(1024)S(1)} %convert_element_type.125) | copy-start | bytes 9220
  74.7 32.3 %copy-start.55 = (f32[3072]{0:T(1024)}, f32[3072]{0:T(1024)S(1)}, u32[]{:S(2)}) copy-start(f32[3072]{0:T(1024)S(1)} %convert_element_type.121) | copy-start | bytes 36868
  89.0 30.0 %copy-start.10 = (f32[576,768]{1,0:T(8,128)}, f32[576,768]{1,0:T(8,128)S(1)}, u32[]{:S(2)}) copy-start(f32[576,768]{1,0:T(8,128)S(1)} %get-tuple-element.67) | copy-start | bytes 5308420
  89.1 30.0 %copy-start.49 = (f32[576]{0:T(1024)}, f32[576]{0:T(1024)S(1)}, u32[]{:S(2)}) copy-start(f32[576]{0:T(1024)S(1)} %broadcast_multiply_fusion.5) | copy-start | bytes 6916
  89.4 29.6 %copy-start.53 = (f32[576]{0:T(1024)}, f32[576]{0:T(1024)S(1)}, u32[]{:S(2)}) copy-start(f32[576]{0:T(1024)S(1)} %add_rsqrt_fusion.1) | copy-start | bytes 6916
  95.3 11.7 %copy-start.69 = (f32[576,3072]{1,0:T(8,128)}, f32[576,3072]{1,0:T(8,128)S(1)}, u32[]{:S(2)}) copy-start(f32[576,3072]{1,0:T(8,128)S(1)} %fusion.88) | copy-start | bytes 21233668
  104.6 10.4 %slice-start.5 = ((s8[4718592]{0:T(1024)(128)(4,1)}), s8[4194304]{0:T(1024)(128)(4,1)S(1)}, s32[]{:S(2)}) async-start(s8[4718592]{0:T(1024)(128)(4,1)} %bitcast.160), calls=%async_computation.18 | async-start | bytes 8388608
  126.3 17.9 %all-to-all-start.1 = ((bf16[576,4,192]{0,2,1:T(8,128)(2,1)}), bf16[576,4,192]{0,2,1:T(8,128)(2,1)S(1)}, u32[]{:S(2)}, u32[]{:S(2)}) async-start(bf16[576,4,192]{0,2,1:T(8,128)(2,1)} %bitcast.7), calls=%async_computation.1 | async-start | bytes 1966080 | tf_op jit(solution)/shard_map/all_to_all | solution.py:183
  130.6 193.6 %all-gather.8.cloned.1.call-start = ((), (), s32[]{:S(2)}) async-start(), calls=%async_computation.8 | async-start | bytes 4423680 | tf_op jit(solution)/shard_map/all_gather | solution.py:225
  131.2 199.5 %all-reduce.5.cloned.1.call-start = ((), (), s32[]{:S(2)}) async-start(), calls=%async_computation.12 | async-start | bytes 4718592 | tf_op jit(solution)/shard_map/psum | solution.py:244
  158.0 9.5 %slice-start = ((s8[12582912]{0:T(1024)(128)(4,1)}), s8[4194304]{0:T(1024)(128)(4,1)S(1)}, s32[]{:S(2)}) async-start(s8[12582912]{0:T(1024)(128)(4,1)} %bitcast.140), calls=%async_computation.13 | async-start | bytes 8388608
  159.1 8.4 %slice-start.1 = ((s8[12582912]{0:T(1024)(128)(4,1)}), s8[4194304]{0:T(1024)(128)(4,1)S(1)}, s32[]{:S(2)}) async-start(s8[12582912]{0:T(1024)(128)(4,1)} %bitcast.140), calls=%async_computation.14 | async-start | bytes 8388608
  159.1 8.6 %slice-start.2 = ((s8[12582912]{0:T(1024)(128)(4,1)}), s8[4194304]{0:T(1024)(128)(4,1)S(1)}, s32[]{:S(2)}) async-start(s8[12582912]{0:T(1024)(128)(4,1)} %bitcast.140), calls=%async_computation.15 | async-start | bytes 8388608
  184.1 258.5 %reduce-scatter.8.cloned.1.call-start = ((), (), s32[]{:S(2)}) async-start(), calls=%async_computation.11 | async-start | bytes 9732096 | tf_op jit(solution)/shard_map/reduce_scatter | solution.py:263
  196.1 388.7 %reduce-scatter.6.cloned.1.call-start = ((), (), s32[]{:S(2)}) async-start(), calls=%async_computation.10 | async-start | bytes 9732096 | tf_op jit(solution)/shard_map/reduce_scatter | solution.py:262
  215.2 8.2 %copy-start.35 = (f32[576]{0:T(1024)S(1)}, f32[576]{0:T(1024)}, u32[]{:S(2)}) copy-start(f32[576]{0:T(1024)} %copy-done.34) | copy-start | bytes 6916
  215.2 8.2 %copy-start.41 = (f32[768]{0:T(1024)S(1)}, f32[768]{0:T(1024)}, u32[]{:S(2)}) copy-start(f32[768]{0:T(1024)} %copy-done.40) | copy-start | bytes 9220
  215.2 8.2 %copy-start.43 = (f32[576]{0:T(1024)S(1)}, f32[576]{0:T(1024)}, u32[]{:S(2)}) copy-start(f32[576]{0:T(1024)} %copy-done.42) | copy-start | bytes 6916
  215.2 8.2 %copy-start.45 = (f32[768]{0:T(1024)S(1)}, f32[768]{0:T(1024)}, u32[]{:S(2)}) copy-start(f32[768]{0:T(1024)} %copy-done.44) | copy-start | bytes 9220
  215.2 67.8 %copy-start.24 = (bf16[256,192]{0,1:T(8,128)(2,1)S(1)}, bf16[256,192]{0,1:T(8,128)(2,1)}, u32[]{:S(2)}) copy-start(bf16[256,192]{0,1:T(8,128)(2,1)} %reshape.222) | copy-start | bytes 294916
  215.2 100.5 %all-to-all-start.2 = ((bf16[3,2304,192]{2,0,1:T(4,128)(2,1)}), bf16[3,2304,192]{2,0,1:T(4,128)(2,1)}, u32[]{:S(2)}, u32[]{:S(2)}) async-start(bf16[3,2304,192]{2,0,1:T(4,128)(2,1)} %copy.139), calls=%async_computation.2 | async-start | bytes 9437184 | tf_op jit(solution)/shard_map/all_to_all | solution.py:224
  222.7 60.6 %copy-start.9 = (bf16[24,8,4,512]{3,1,2,0:T(8,128)(2,1)S(1)}, bf16[24,8,4,512]{3,1,2,0:T(8,128)(2,1)}, u32[]{:S(2)}) copy-start(bf16[24,8,4,512]{3,1,2,0:T(8,128)(2,1)} %copy-done.8) | copy-start | bytes 2359300
  315.7 8.6 %copy-start.4 = (f32[576,768]{1,0:T(8,128)S(1)}, f32[576,768]{1,0:T(8,128)}, u32[]{:S(2)}) copy-start(f32[576,768]{1,0:T(8,128)} %copy-done.3) | copy-start | bytes 5308420
  330.7 256.9 %copy-start.27 = (f32[192,768]{1,0:T(8,128)S(1)}, f32[192,768]{1,0:T(8,128)}, u32[]{:S(2)}) copy-start(f32[192,768]{1,0:T(8,128)} %get-tuple-element.86) | copy-start | bytes 1769476
  (56 other events, 228.8 us)
Sparse Core Ops, SparseCore 0:
  9.6 33.2 all-gather.3
  44.4 17.4 all-gather.5
  122.8 34.8 reduce-scatter.3
  159.2 30.9 all-gather.7
  194.1 108.0 all-reduce.4
  308.5 134.0 reduce-scatter.7
  450.1 134.5 reduce-scatter.5
where the time goes:
time: 607 us; the launch traced here: 596 us
  waiting for transfers between devices  312 us (51%)
  matrix products  95.6 us (16%)
  blocking collectives  90 us (15%)
  local copies, waits for them, and re-layouts  45.5 us (7%)
  other arithmetic  20.1 us (3%)
  between operations  16.5 us (3%)
  starting transfers between devices  15.9 us (3%)
    reduce_scatter x1, waiting for transfers between devices, shards(): lax.psum_scatter(grad_w_in, ('dp', 'head'), scatter_dimension=1, tiled=True)  142 us
    reduce_scatter x1, waiting for transfers between devices, shards(): lax.psum_scatter(grad_w_down, ('dp', 'head'), scatter_dimension=0, tiled=...  112 us
    psum x1, blocking collectives, shards(): lax.psum((grad_b_out, grad_gain_one, grad_shift_one, grad_b_in, grad_b_do...  57.7 us
    psum x1, blocking collectives, shards(): lax.psum((grad_w_qkv, grad_b_qv, grad_w_out, vectors[0], vectors[1], vect...  32.2 us
    all_gather x1, waiting for transfers between devices, shards(): gathered = lax.all_gather(tokens, 'head', axis=0, tiled=True)  31.8 us
    unnamed x163, local copies, waits for them, and re-layouts  13.4 us
    all_to_all x1, waiting for transfers between devices, shards(): lax.all_to_all(grad_context_local, 'head', split_axis=1, concat_axis=0, t...  12.2 us
  transfers between devices with their start and end apart: 10, of which 5 were waited for; matrix products, arithmetic and copies ran while one was open for 19% of the time, Pallas kernels for 0%

commit v1 on v0

v1 whole, which is shorter than its diff:
```python
import math

import jax
import jax.numpy as jnp
from jax import lax
from jax.sharding import PartitionSpec as P

HEAD_DIM = 64
PLEN = 512
QLEN = 32
F32 = jnp.float32
BF16 = jnp.bfloat16


def swap(array, axis, bit):
    size = lax.axis_size(axis)
    return lax.ppermute(array, axis, [(at, at ^ bit) for at in range(size)])


def bits_of(size):
    return [1 << at for at in range(size.bit_length() - 1)]


def align(rows, extra):
    heads = lax.axis_size("head")
    me = lax.axis_index("head")
    count = rows.shape[0]
    last = heads - 1
    moved = extra * last
    payload = jnp.where(me == last, rows[count - moved - extra : count - extra], rows[count - moved :])
    received = lax.ppermute(payload, "head", [(at, (at + 1) % heads) for at in range(heads)])
    passage = lax.dynamic_slice_in_dim(
        jnp.concatenate([received, rows], 0), moved - extra * me, count - extra, 0
    )
    query = jnp.where(me == 0, received[:extra], rows[count - extra :])
    for target in range(1, last):
        begin = count - (heads - target) * extra
        sent = lax.ppermute(rows[begin : begin + extra], "head", [(last, target)])
        query = jnp.where(me == target, sent, query)
    return jnp.concatenate([passage, query], 0)


def unalign(rows, extra):
    heads = lax.axis_size("head")
    me = lax.axis_index("head")
    count = rows.shape[0]
    last = heads - 1
    moved = extra * last
    query = rows[count - extra :]
    payload = jnp.where(
        me == 0, jnp.concatenate([query, rows[: moved - extra]], 0), rows[:moved]
    )
    received = lax.ppermute(payload, "head", [((at + 1) % heads, at) for at in range(heads)])
    queries = [received[:extra]]
    for source in range(1, last):
        queries.append(lax.ppermute(query, "head", [(source, last)]))
    queries.append(query)
    tail = jnp.where(
        me == last,
        jnp.concatenate(queries, 0),
        jnp.concatenate([received, query], 0),
    )
    return lax.dynamic_slice_in_dim(
        jnp.concatenate([rows[: count - extra], tail], 0), extra * me, count, 0
    )


def split_three(values):
    high = lax.reduce_precision(values, 8, 7)
    rest = values - high
    middle = lax.reduce_precision(rest, 8, 7)
    return [part.astype(BF16) for part in (high, middle, rest - middle)]


def with_column(rows, values):
    parts = jnp.stack(split_three(values), 1)
    return jnp.concatenate([rows, jnp.pad(parts, ((0, 0), (0, 125)))], 1)


def column_of(rows, width):
    parts = rows[:, width : width + 3].astype(F32)
    return rows[:, :width], parts[:, 0] + (parts[:, 1] + parts[:, 2])


def scatter_sum(current, order):
    axes = dict(order)
    remaining = [name for name, _ in sorted(order, key=lambda item: item[1][2])]
    for name, (axis, bit, _) in order:
        at = remaining.index(name)
        keep = lax.index_in_dim(current, 0, at, keepdims=False)
        send = lax.index_in_dim(current, 1, at, keepdims=False).astype(BF16)
        current = keep + swap(send, axis, bit).astype(F32)
        remaining.remove(name)
    return current


def relative(array, axis, bit, at):
    mine = (lax.axis_index(axis) & bit) != 0
    return jnp.where(mine, jnp.flip(array, at), array)


def attention_scores(query, keys, valid):
    scores = jnp.einsum("qhd,khd->hqk", query, keys, preferred_element_type=F32) * (
        1.0 / math.sqrt(HEAD_DIM)
    )
    return jnp.where(valid[None], scores, -1000000000.0)


def attend(query, keys, values, valid):
    scores = attention_scores(query, keys, valid)
    row_max = jnp.max(scores, -1, keepdims=True)
    exponent = jnp.exp(scores - row_max)
    total = jnp.sum(exponent, -1, keepdims=True)
    shares = (exponent / total).astype(BF16)
    mixed = jnp.einsum("hqk,khd->qhd", shares, values, preferred_element_type=F32).astype(BF16)
    return mixed, row_max + jnp.log(total)


def attend_back(query, keys, values, valid, log_total, grad_mixed):
    scores = attention_scores(query, keys, valid)
    shares = jnp.exp(scores - log_total)
    grad_shares = jnp.einsum("qhd,khd->hqk", grad_mixed, values, preferred_element_type=F32)
    grad_values = jnp.einsum(
        "hqk,qhd->khd", shares.astype(BF16), grad_mixed, preferred_element_type=F32
    ).astype(BF16)
    inner = jnp.sum(shares * grad_shares, -1, keepdims=True)
    grad_scores = (shares * (grad_shares - inner)).astype(BF16)
    scale = 1.0 / math.sqrt(HEAD_DIM)
    grad_query = jnp.einsum("hqk,khd->qhd", grad_scores, keys, preferred_element_type=F32) * scale
    grad_keys = jnp.einsum("hqk,qhd->khd", grad_scores, query, preferred_element_type=F32) * scale
    return grad_query.astype(BF16), grad_keys.astype(BF16), grad_values


def normalize(hidden, gain, shift):
    center = hidden - jnp.mean(hidden, -1, keepdims=True)
    inverse = lax.rsqrt(jnp.mean(center * center, -1, keepdims=True) + 1e-06)
    unit = center * inverse
    return (unit * gain + shift, unit, inverse)


def normalize_back(grad, unit, inverse, gain):
    grad_unit = grad * gain
    return inverse * (
        grad_unit
        - jnp.mean(grad_unit, -1, keepdims=True)
        - unit * jnp.mean(grad_unit * unit, -1, keepdims=True)
    )


def shards(
    tokens, w_qkv, b_qv, w_out, b_out, gain_one, shift_one, w_in, b_in, w_down, b_down,
    gain_two, shift_two, w_term, b_term, pass_len, query_len, grad_out, grad_term,
):
    n_dp, n_head = lax.axis_size("dp"), lax.axis_size("head")
    me = lax.axis_index("head")
    width = tokens.shape[1]
    wide = w_qkv.shape[2]
    hidden = w_in.shape[1]
    extra = query_len.shape[0] * QLEN // n_head
    split = PLEN

    own_pack = jnp.concatenate([w_qkv.transpose(0, 2, 1).reshape(3 * wide, width), w_out], 0)
    rows = align(tokens, extra)
    packs = [own_pack, swap(own_pack, "head", 1)]
    packs.append(swap(own_pack, "head", 2))
    packs.append(swap(packs[2], "head", 1))
    bias = jnp.concatenate([b_qv, jnp.zeros_like(b_qv)], 0).reshape(1, -1)
    all_bias = lax.all_to_all(
        jnp.tile(b_qv.reshape(1, 2, wide), (n_head, 1, 1)), "head", 0, 0, tiled=True
    )
    length = lax.dynamic_index_in_dim(pass_len, me, 0, keepdims=False)
    each = query_len.shape[0] // n_head
    lengths = lax.dynamic_slice_in_dim(query_len, me * each, each, 0)
    long_valid = jnp.broadcast_to(
        jnp.arange(PLEN, dtype=jnp.int32)[None, :] < length, (PLEN, PLEN)
    )
    place = jnp.arange(extra, dtype=jnp.int32)
    short_valid = (place[:, None] // QLEN == place[None, :] // QLEN) & (
        place[None, :] % QLEN < lengths[place // QLEN][None, :]
    )
    grads_in = align(with_column(grad_out, grad_term), extra)

    saved = []
    attention = b_out.astype(F32)[None, :]
    for part in range(n_head):
        pack = packs[part]
        owner_bias = lax.dynamic_index_in_dim(all_bias, me ^ part, 0, keepdims=False).astype(F32)
        both = jnp.einsum("td,ed->te", rows, pack[: 3 * wide], preferred_element_type=F32)
        query = (both[:, :wide] + owner_bias[0]).astype(BF16).reshape(-1, wide // HEAD_DIM, HEAD_DIM)
        keys = both[:, wide : 2 * wide].astype(BF16).reshape(-1, wide // HEAD_DIM, HEAD_DIM)
        values = (both[:, 2 * wide :] + owner_bias[1]).astype(BF16).reshape(
            -1, wide // HEAD_DIM, HEAD_DIM
        )
        long_mixed, long_total = attend(query[:split], keys[:split], values[:split], long_valid)
        short_mixed, short_total = attend(query[split:], keys[split:], values[split:], short_valid)
        mixed = jnp.concatenate([long_mixed, short_mixed], 0).reshape(-1, wide)
        attention = attention + jnp.dot(mixed, pack[3 * wide :], preferred_element_type=F32)
        saved.append((query, keys, values, mixed, long_total, short_total))

    gain_first = gain_one.astype(F32)
    gain_second = gain_two.astype(F32)
    residual = rows.astype(F32) + attention
    first, first_unit, first_inverse = normalize(residual, gain_first, shift_one.astype(F32))
    first_low = first.astype(BF16)
    inner = jnp.dot(first_low, w_in, preferred_element_type=F32) + b_in.astype(F32)
    active, gelu_back = jax.vjp(jax.nn.gelu, inner)
    active_low = active.astype(BF16)
    second_in = (
        first + jnp.dot(active_low, w_down, preferred_element_type=F32) + b_down.astype(F32)
    )
    second, second_unit, second_inverse = normalize(second_in, gain_second, shift_two.astype(F32))
    term_weight = w_term.astype(F32)
    logit = jnp.sum(second * term_weight[None, :], -1) + b_term.astype(F32)[0]
    term = jax.nn.softplus(logit)
    rows_out = unalign(with_column(second.astype(BF16), term), extra)
    out, term = column_of(rows_out, width)

    grad_second, grad_weight = column_of(grads_in, width)
    grad_logit = grad_weight * jax.nn.sigmoid(logit)
    grad_w_term = jnp.sum(grad_logit[:, None] * second, 0)
    grad_b_term = jnp.sum(grad_logit)[None]
    grad_second = grad_second.astype(F32) + grad_logit[:, None] * term_weight[None, :]
    grad_gain_two = jnp.sum(grad_second * second_unit, 0)
    grad_shift_two = jnp.sum(grad_second, 0)
    grad_middle = normalize_back(grad_second, second_unit, second_inverse, gain_second)
    grad_b_down = jnp.sum(grad_middle, 0)
    grad_middle_low = grad_middle.astype(BF16)

    def owned(grad):
        dp_bits = bits_of(n_dp)[::-1]
        shape = [2] * len(dp_bits) + [2, 2]
        current = grad.reshape(*shape, hidden // (n_dp * n_head), width)
        for at, bit in enumerate(dp_bits):
            current = relative(current, "dp", bit, at)
        current = relative(current, "head", 2, len(dp_bits))
        return relative(current, "head", 1, len(dp_bits) + 1)

    stages = {}
    for at, bit in enumerate(bits_of(n_dp)[::-1]):
        stages["dp%d" % bit] = ("dp", bit, at)
    stages["x"] = ("head", 2, len(stages))
    stages["core"] = ("head", 1, len(stages))
    dp_names = ["dp%d" % bit for bit in bits_of(n_dp)]
    order_x = [(name, stages[name]) for name in ["core", "x"] + dp_names]
    order_y = [(name, stages[name]) for name in ["core", dp_names[0], "x"] + dp_names[1:]]

    grad_w_down = jnp.einsum("tf,td->fd", active_low, grad_middle_low, preferred_element_type=F32)
    grad_w_down = scatter_sum(owned(grad_w_down), order_x)
    grad_active = jnp.einsum("td,fd->tf", grad_middle_low, w_down, preferred_element_type=F32)
    grad_inner = gelu_back(grad_active)[0]
    grad_b_in = jnp.sum(grad_inner, 0)
    grad_inner_low = grad_inner.astype(BF16)
    grad_w_in = jnp.einsum("tf,td->fd", grad_inner_low, first_low, preferred_element_type=F32)
    grad_w_in = scatter_sum(owned(grad_w_in), order_y).T
    grad_first = grad_middle + jnp.einsum(
        "tf,df->td", grad_inner_low, w_in, preferred_element_type=F32
    )
    grad_gain_one = jnp.sum(grad_first * first_unit, 0)
    grad_shift_one = jnp.sum(grad_first, 0)
    grad_residual = normalize_back(grad_first, first_unit, first_inverse, gain_first)
    grad_b_out = jnp.sum(grad_residual, 0)
    grad_attention = grad_residual.astype(BF16)

    sums = [
        grad_b_out, grad_gain_one, grad_shift_one, grad_b_in, grad_b_down, grad_gain_two,
        grad_shift_two, grad_w_term, jnp.pad(grad_b_term, (0, 127)),
    ]
    sizes = [member.shape[0] for member in sums]
    vector = jnp.concatenate(sums)
    for axis, bit in [("head", 1), ("head", 2)] + [("dp", bit) for bit in bits_of(n_dp)]:
        vector = vector + swap(vector, axis, bit)
    cuts = [sum(sizes[:at]) for at in range(1, len(sizes))]
    vectors = jnp.split(vector, cuts)

    grad_packs, grad_biases = [None] * n_head, [None] * n_head
    grad_rows = grad_residual
    for part in (3, 2, 1, 0):
        pack = packs[part]
        query, keys, values, mixed, long_total, short_total = saved[part]
        grad_mixed = jnp.einsum(
            "td,ed->te", grad_attention, pack[3 * wide :], preferred_element_type=F32
        ).astype(BF16).reshape(-1, wide // HEAD_DIM, HEAD_DIM)
        long_grads = attend_back(
            query[:split], keys[:split], values[:split], long_valid, long_total, grad_mixed[:split]
        )
        short_grads = attend_back(
            query[split:], keys[split:], values[split:], short_valid, short_total, grad_mixed[split:]
        )
        grads = jnp.concatenate(
            [
                jnp.concatenate([long_grads[at], short_grads[at]], 0).reshape(-1, wide)
                for at in range(3)
            ],
            1,
        )
        grad_biases[part] = jnp.stack(
            [
                jnp.sum(grads[:, :wide], 0, dtype=F32),
                jnp.sum(grads[:, 2 * wide :], 0, dtype=F32),
            ]
        )
        grad_packs[part] = jnp.concatenate(
            [
                jnp.einsum("te,td->ed", grads, rows, preferred_element_type=F32),
                jnp.einsum("te,td->ed", mixed, grad_attention, preferred_element_type=F32),
            ],
            0,
        )
        grad_rows = grad_rows + jnp.dot(grads, pack[: 3 * wide], preferred_element_type=F32)
    grad_tokens = unalign(grad_rows.astype(BF16), extra)

    far = grad_packs[2] + swap(grad_packs[3].astype(BF16), "head", 1).astype(F32)
    near = grad_packs[0] + swap(grad_packs[1].astype(BF16), "head", 1).astype(F32)
    block = near + swap(far.astype(BF16), "head", 2).astype(F32)
    far_bias = grad_biases[2] + swap(grad_biases[3], "head", 1)
    near_bias = grad_biases[0] + swap(grad_biases[1], "head", 1)
    grad_b_qv = near_bias + swap(far_bias, "head", 2)
    for bit in bits_of(n_dp):
        grad_b_qv = grad_b_qv + swap(grad_b_qv, "dp", bit)
    me_dp = lax.axis_index("dp")
    for bit in bits_of(n_dp):
        half = block.shape[0] // 2
        side = ((me_dp & bit) != 0).astype(jnp.int32)
        keep = lax.dynamic_slice_in_dim(block, side * half, half, 0)
        send = lax.dynamic_slice_in_dim(block, (1 - side) * half, half, 0).astype(BF16)
        block = keep + swap(send, "dp", bit).astype(F32)
    block = block.astype(BF16)
    for bit in bits_of(n_dp)[::-1]:
        other = swap(block, "dp", bit)
        mine = (me_dp & bit) != 0
        block = jnp.where(
            mine, jnp.concatenate([other, block], 0), jnp.concatenate([block, other], 0)
        )
    block = block.astype(F32)
    grad_w_qkv = block[: 3 * wide].reshape(3, wide, width).transpose(0, 2, 1)
    grad_w_out = block[3 * wide :]
    return (
        out, term, grad_tokens, grad_w_qkv, grad_b_qv, grad_w_out, vectors[0], vectors[1],
        vectors[2], grad_w_in, vectors[3], grad_w_down, vectors[4], vectors[5], vectors[6],
        vectors[7], vectors[8][:1],
    )


def solution(mesh):
    both = ("dp", "head")
    placed = (
        P(both, None), P(None, None, "head"), P(None, "head"), P("head", None),
        P(), P(), P(), P(), P(), P(), P(), P(), P(), P(), P(),
        P("dp"), P("dp"), P(both, None), P(both),
    )
    return jax.shard_map(
        shards,
        mesh=mesh,
        in_specs=placed,
        out_specs=(
            P(both, None), P(both), P(both, None), P(None, None, "head"), P(None, "head"),
            P("head", None), P(), P(), P(), P(None, both), P(), P(both, None),
            P(), P(), P(), P(), P(),
        ),
        check_vma=False,
    )
```

time: 607 us -> 454 us (0.75)
  waiting for transfers between devices: 312 us -> 99.6 us
  other arithmetic: 20.1 us -> 116 us
  blocking collectives: 90 us -> 0 us
  starting transfers between devices: 15.9 us -> 54 us
  matrix products: 95.6 us -> 117 us
  between operations: 16.5 us -> 4.82 us
  local copies, waits for them, and re-layouts: 45.5 us -> 57.1 us
    reduce_scatter x3 -> x0, waiting for transfers between devices: 254 us -> none  [the longest x1 142 us: shards(): lax.psum_scatter(grad_w_in, ('dp', 'head'), scatter_dimension=1, tiled=True)]
    psum x2 -> x0, blocking collectives: 90 us -> none  [the longest x1 57.7 us: shards(): lax.psum((grad_b_out, grad_gain_one, grad_shift_one, grad_b_in, grad_b_do...]
    ppermute x0 -> x45, waiting for transfers between devices: none -> 89.4 us  [the longest x33 58.5 us: swap(): return lax.ppermute(array, axis, [(at, at ^ bit) for at in range(size)])]
    select_n x0 -> x21, other arithmetic: none -> 49.6 us  [the longest x10 39.3 us: relative(): return jnp.where(mine, jnp.flip(array, at), array)]
    ppermute x0 -> x45, starting transfers between devices: none -> 49.2 us  [the longest x33 35.8 us: swap(): return lax.ppermute(array, axis, [(at, at ^ bit) for at in range(size)])]
    all_gather x3 -> x0, waiting for transfers between devices: 31.9 us -> none  [the longest x1 31.8 us: shards(): gathered = lax.all_gather(tokens, 'head', axis=0, tiled=True)]
    dot_general x25 -> x77, matrix products: 83.8 us -> 109 us  [the longest x1 11.8 us: shards(): jnp.einsum('td,fd->tf', grad_middle_low, w_down, preferred_element_type=F32)]
    add x2 -> x33, other arithmetic: 0.65 us -> 21.7 us  [the longest x9 11.3 us: scatter_sum(): current = keep + swap(send, axis, bit).astype(F32)]
  transfers between devices with their start and end apart: 10 -> 46, of which waited for: 5 -> 19; matrix products, arithmetic and copies ran while one was open for 19% -> 31% of each run, Pallas kernels for 0% -> 0%
where the time goes in v1:
time: 454 us; the launch traced here: 448 us
  matrix products  117 us (26%)
  other arithmetic  116 us (26%)
  waiting for transfers between devices  99.6 us (22%)
  local copies, waits for them, and re-layouts  57.1 us (13%)
  starting transfers between devices  54 us (12%)
  between operations  4.82 us (1%)
    ppermute x33, waiting for transfers between devices, swap(): return lax.ppermute(array, axis, [(at, at ^ bit) for at in range(size)])  58.5 us
    select_n x10, other arithmetic, relative(): return jnp.where(mine, jnp.flip(array, at), array)  39.3 us
    ppermute x33, starting transfers between devices, swap(): return lax.ppermute(array, axis, [(at, at ^ bit) for at in range(size)])  35.8 us
    ppermute x4, waiting for transfers between devices, unalign(): queries.append(lax.ppermute(query, 'head', [(source, last)]))  25.7 us
    unnamed x384, local copies, waits for them, and re-layouts  20.3 us
    dot_general x1, matrix products, shards(): jnp.einsum('td,fd->tf', grad_middle_low, w_down, preferred_element_type=F32)  11.8 us
    add x9, other arithmetic, scatter_sum(): current = keep + swap(send, axis, bit).astype(F32)  11.3 us
    all_to_all x1, waiting for transfers between devices, shards(): lax.all_to_all(jnp.tile(b_qv.reshape(1, 2, wide), (n_head, 1, 1)), 'head'...  10.1 us
  transfers between devices with their start and end apart: 46, of which 19 were waited for; matrix products, arithmetic and copies ran while one was open for 31% of the time, Pallas kernels for 0%

profile of v1, /device:TPU:1, one launch (start us, length us, event | category | flops | bytes accessed | tf_op | source)
XLA Modules:
  0.0 448.3 jit_solution(10688437659670087524)
XLA Ops:
  11.7 4.8 %all-to-all-start = ((bf16[4,2,192]{2,1,0:T(2,128)(2,1)}), bf16[4,2,192]{2,1,0:T(2,128)(2,1)S(1)}, u32[]{:S(2)}, u32[]{:S(2)}) async-start(bf16[4,2,192]{2,1,0:T(2,128)(2,1)} %tile.2), calls=%async_computation | async-start | bytes 8192 | tf_op jit(solution)/shard_map/all_to_all | solution.py:168
  28.1 10.1 %all-to-all-done = bf16[4,2,192]{2,1,0:T(2,128)(2,1)S(1)} async-done(((bf16[4,2,192]{2,1,0:T(2,128)(2,1)}), bf16[4,2,192]{2,1,0:T(2,128)(2,1)S(1)}, u32[]{:S(2)}, u32[]{:S(2)}) %all-to-all-start) | async-done | bytes 3104 | tf_op jit(solution)/shard_map/all_to_all | solution.py:168
  61.3 4.3 collective-permute-start.5
  77.0 5.4 %fusion.258 = f32[576,3072]{1,0:T(8,128)} fusion(bf16[768,3072]{1,0:T(8,128)(2,1)S(1)} %bitcast.323, f32[576,768]{0,1:T(8,128)S(1)} %get-tuple-element.115, f32[768]{0:T(1024)S(1)} %copy-done.122, f32[768]{0:T(1024)S(1)} %copy-done.117, f32[576]{0:T(1024)S(1)} %add_rsqrt_fusion.1, f32[576]{0:T(1024)S(1)} %broadcast_multiply_fusion.5), kind=kOutput, calls=%fused_computation.508 | convolution fusion | flops 2720120832 | bytes 13576704 | tf_op jit(solution)/shard_map/dot_general | solution.py:205
  82.4 8.8 %fusion.285 = (f32[576]{0:T(1024)S(1)}, f32[576,768]{0,1:T(8,128)S(1)}) fusion(f32[768]{0:T(1024)S(1)} %copy-done.160, bf16[3072,768]{1,0:T(8,128)(2,1)} %param.28, f32[576,3072]{1,0:T(8,128)} %fusion.258, f32[3072]{0:T(1024)S(1)} %copy-done.149, f32[768]{0:T(1024)S(1)} %copy-done.122, f32[768]{0:T(1024)S(1)} %copy-done.117, f32[576]{0:T(1024)S(1)} %add_rsqrt_fusion.1, ...), kind=kOutput, calls=%fused_computation.533 | convolution fusion | flops 2738699776 | bytes 15363840 | tf_op jit(solution)/shard_map/dot_general | solution.py:209
  98.3 11.8 %fusion.286 = (f32[3072]{0:T(1024)}, bf16[576,3072]{1,0:T(8,128)(2,1)}) fusion(f32[576,3072]{1,0:T(8,128)S(1)} %bitcast.316, f32[3072]{0:T(1024)S(1)} %copy-done.149, bf16[3072,768]{1,0:T(8,128)(2,1)} %param.28, f32[576,768]{0,1:T(8,128)S(1)} %get-tuple-element.46), kind=kOutput, calls=%fused_computation.534 | convolution fusion | flops 2757276672 | bytes 17129472 | tf_op jit(solution)/shard_map/td,fd->tf/dot_general | solution.py:249
  110.2 7.0 %multiply_reduce_fusion.6 = (f32[768]{0:T(1024)}, f32[576]{0:T(1024)S(1)}, f32[576]{0:T(1024)S(1)}, f32[768]{0:T(1024)}, f32[576,768]{0,1:T(8,128)S(1)}) fusion(f32[576,768]{0,1:T(8,128)S(1)} %get-tuple-element.115, f32[576]{0:T(1024)S(1)} %add_rsqrt_fusion.1, f32[576]{0:T(1024)S(1)} %broadcast_multiply_fusion.5, f32[768]{0:T(1024)S(1)} %copy-done.117, ...), kind=kOutput, calls=%fused_computation.75 | convolution fusion | flops 2722330112 | bytes 13584384 | tf_op jit(solution)/shard_map/tf,df->td/dot_general | solution.py:255
  191.3 6.8 %fusion.25 = f32[3072,768]{1,0:T(8,128)} fusion(bf16[576,3072]{1,0:T(8,128)(2,1)S(1)} %copy-done.174, f32[576,768]{0,1:T(8,128)S(1)} %get-tuple-element.115, f32[768]{0:T(1024)S(1)} %copy-done.123, f32[768]{0:T(1024)S(1)} %copy-done.118, f32[576]{0:T(1024)S(1)} %copy-done.131, f32[576]{0:T(1024)S(1)} %copy-done.125), kind=kOutput, calls=%fused_computation.97 | convolution fusion | flops 2720120832 | bytes 14756352 | tf_op jit(solution)/shard_map/tf,td->fd/dot_general | solution.py:253
  198.2 7.9 %fusion.161 = f32[3072,768]{1,0:T(8,128)} fusion(f32[576,768]{0,1:T(8,128)S(1)} %copy-done.31, f32[576,3072]{1,0:T(8,128)S(1)} %bitcast.318, f32[3072]{0:T(1024)S(1)} %copy-done.150), kind=kOutput, calls=%fused_computation.306 | convolution fusion | flops 2736046080 | bytes 18296832 | tf_op jit(solution)/shard_map/tf,td->fd/dot_general | solution.py:247
  226.4 4.8 %copy.336 = f32[2,2,2,2,2,96,768]{6,5,0,1,2,3,4:T(8,128)S(1)} copy(f32[2,2,2,2,2,96,768]{6,5,4,3,2,1,0:T(8,128)} %bitcast.314) | data formatting | bytes 18874368 | tf_op jit(solution)/shard_map/reshape | solution.py:232
  234.4 4.7 %copy.339 = f32[2,2,2,2,2,96,768]{6,5,0,1,2,3,4:T(8,128)S(1)} copy(f32[2,2,2,2,2,96,768]{6,5,4,3,2,1,0:T(8,128)} %bitcast.313) | data formatting | bytes 18874368 | tf_op jit(solution)/shard_map/reshape | solution.py:232
  239.1 4.8 %reverse_select_fusion.4 = f32[2,2,2,2,2,96,768]{6,5,0,1,2,3,4:T(8,128)} fusion(f32[2,2,2,2,2,96,768]{6,5,0,1,2,3,4:T(8,128)S(1)} %copy.339, pred[]{:T(512)S(6)} %ne.146), kind=kLoop, calls=%fused_computation.4 | loop fusion | flops 2359296 | bytes 18874368 | tf_op jit(solution)/shard_map/jit(_where)/select_n | solution.py:99
  243.9 8.2 %reverse_select_fusion.3 = f32[2,2,2,2,2,96,768]{6,5,0,1,2,3,4:T(8,128)S(1)} fusion(f32[2,2,2,2,2,96,768]{6,5,0,1,2,3,4:T(8,128)} %reverse_select_fusion.4, pred[]{:T(512)S(6)} %ne.145), kind=kLoop, calls=%fused_computation.3 | loop fusion | flops 2359296 | bytes 18874368 | tf_op jit(solution)/shard_map/jit(_where)/select_n | solution.py:99
  252.2 4.6 %reverse_select_fusion.2 = f32[2,2,2,2,2,96,768]{6,5,0,1,2,3,4:T(8,128)} fusion(f32[2,2,2,2,2,96,768]{6,5,0,1,2,3,4:T(8,128)S(1)} %reverse_select_fusion.3, pred[]{:T(512)S(6)} %ne.144), kind=kLoop, calls=%fused_computation.2 | loop fusion | flops 2359296 | bytes 18874368 | tf_op jit(solution)/shard_map/jit(_where)/select_n | solution.py:99
  256.8 4.8 %reverse_select_fusion.6 = f32[2,2,2,2,2,96,768]{6,5,0,1,2,3,4:T(8,128)} fusion(f32[2,2,2,2,2,96,768]{6,5,0,1,2,3,4:T(8,128)S(1)} %reverse_select_fusion.7, pred[]{:T(512)S(6)} %ne.148), kind=kLoop, calls=%fused_computation.6 | loop fusion | flops 2359296 | bytes 18874368 | tf_op jit(solution)/shard_map/jit(_where)/select_n | solution.py:99
  261.6 8.0 %reverse_select_fusion.1 = f32[2,2,2,2,2,96,768]{6,5,0,1,2,3,4:T(8,128)S(1)} fusion(f32[2,2,2,2,2,96,768]{6,5,0,1,2,3,4:T(8,128)} %reverse_select_fusion.2, pred[]{:T(512)S(6)} %ne.148), kind=kLoop, calls=%fused_computation.1 | loop fusion | flops 2359296 | bytes 18874368 | tf_op jit(solution)/shard_map/jit(_where)/select_n | solution.py:99
  270.7 4.6 %reverse_select_fusion.5 = f32[2,2,2,2,2,96,768]{6,5,0,1,2,3,4:T(8,128)} fusion(f32[2,2,2,2,2,96,768]{6,5,0,1,2,3,4:T(8,128)S(1)} %copy-done, pred[]{:T(512)S(6)} %ne.147), kind=kLoop, calls=%fused_computation.5 | loop fusion | flops 2359296 | bytes 18874368 | tf_op jit(solution)/shard_map/jit(_where)/select_n | solution.py:99
  276.4 7.5 %fusion.16 = bf16[2,2,2,2,96,768]{5,4,0,1,2,3:T(8,128)(2,1)} fusion(f32[2,2,2,2,2,96,768]{6,5,0,1,2,3,4:T(8,128)} %reverse_select_fusion.5), kind=kLoop, calls=%fused_computation.57 | loop fusion | bytes 4718592 | tf_op jit(solution)/shard_map/convert_element_type | solution.py:91
  297.7 3.2 collective-permute-start.15
  311.1 25.5 %collective-permute-done.13 = bf16[64,768]{0,1:T(8,128)(2,1)S(1)} collective-permute-done((bf16[64,768]{0,1:T(8,128)(2,1)}, bf16[64,768]{0,1:T(8,128)(2,1)S(1)}, u32[]{:S(2)}, u32[]{:S(2)}) %collective-permute-start.13) | collective-permute-done | bytes 98336 | tf_op jit(solution)/shard_map/ppermute | solution.py:56
  336.6 3.7 collective-permute-done.34
  348.2 5.2 %collective-permute-done.6 = bf16[192,896]{0,1:T(8,128)(2,1)S(1)} collective-permute-done((bf16[192,896]{0,1:T(8,128)(2,1)S(1)}, bf16[192,896]{0,1:T(8,128)(2,1)S(1)}, u32[]{:S(2)}, u32[]{:S(2)}) %collective-permute-start.6) | collective-permute-done | bytes 344096 | tf_op jit(solution)/shard_map/ppermute | solution.py:53
  364.2 3.8 fusion.7
  369.9 9.6 %collective-permute-done.18 = bf16[384,768]{1,0:T(8,128)(2,1)S(1)} collective-permute-done((bf16[384,768]{1,0:T(8,128)(2,1)S(1)}, bf16[384,768]{1,0:T(8,128)(2,1)S(1)}, u32[]{:S(2)}, u32[]{:S(2)}) %collective-permute-start.18) | collective-permute-done | bytes 589856 | tf_op jit(solution)/shard_map/ppermute | solution.py:17
  382.2 3.5 collective-permute-done.19
  385.9 3.3 collective-permute-start.41
  389.2 6.0 %collective-permute-done.20 = bf16[96,768]{1,0:T(8,128)(2,1)S(1)} collective-permute-done((bf16[96,768]{1,0:T(8,128)(2,1)S(1)}, bf16[96,768]{1,0:T(8,128)(2,1)S(1)}, u32[]{:S(2)}, u32[]{:S(2)}) %collective-permute-start.20) | collective-permute-done | bytes 147488 | tf_op jit(solution)/shard_map/ppermute | solution.py:17
  407.4 8.1 %collective-permute-done.41 = bf16[2,2,2,96,768]{4,3,0,1,2:T(8,128)(2,1)} collective-permute-done((bf16[2,2,2,96,768]{4,3,0,1,2:T(8,128)(2,1)S(1)}, bf16[2,2,2,96,768]{4,3,0,1,2:T(8,128)(2,1)}, u32[]{:S(2)}, u32[]{:S(2)}) %collective-permute-start.41) | collective-permute-done | bytes 1179680 | tf_op jit(solution)/shard_map/ppermute | solution.py:17
  419.0 4.3 collective-permute-done.37
  423.6 6.3 %collective-permute-done.42 = bf16[2,2,96,768]{3,2,0,1:T(8,128)(2,1)S(1)} collective-permute-done((bf16[2,2,96,768]{3,2,0,1:T(8,128)(2,1)S(1)}, bf16[2,2,96,768]{3,2,0,1:T(8,128)(2,1)S(1)}, u32[]{:S(2)}, u32[]{:S(2)}) %collective-permute-start.42) | collective-permute-done | bytes 589856 | tf_op jit(solution)/shard_map/ppermute | solution.py:17
  431.5 4.7 %collective-permute-done.23 = bf16[384,768]{1,0:T(8,128)(2,1)S(1)} collective-permute-done((bf16[384,768]{1,0:T(8,128)(2,1)S(1)}, bf16[384,768]{1,0:T(8,128)(2,1)S(1)}, u32[]{:S(2)}, u32[]{:S(2)}) %collective-permute-start.23) | collective-permute-done | bytes 589856 | tf_op jit(solution)/shard_map/ppermute | solution.py:17
  441.5 4.2 collective-permute-done.39
  (763 shorter events, 232.9 us)
Async XLA Ops:
  3.1 47.2 %collective-permute-start.4 = (bf16[768,768]{1,0:T(8,128)(2,1)}, bf16[768,768]{1,0:T(8,128)(2,1)}, u32[]{:S(2)}, u32[]{:S(2)}) collective-permute-start(bf16[768,768]{1,0:T(8,128)(2,1)} %pad_maximum_fusion), channel_id=1, source_target_pairs={{0,2},{1,3},{2,0},{3,1},{4,6},{5,7},{6,4},{7,5},{8,10},{9,11},{10,... | collective-permute-start | bytes 3538952 | tf_op jit(solution)/shard_map/ppermute | solution.py:17
  5.1 47.4 %collective-permute-start.3 = (bf16[768,768]{1,0:T(8,128)(2,1)}, bf16[768,768]{1,0:T(8,128)(2,1)}, u32[]{:S(2)}, u32[]{:S(2)}) collective-permute-start(bf16[768,768]{1,0:T(8,128)(2,1)} %pad_maximum_fusion), channel_id=1, source_target_pairs={{0,1},{1,0},{2,3},{3,2},{4,5},{5,4},{6,7},{7,6},{8,9},{9,8},{10,11... | collective-permute-start | bytes 3538952 | tf_op jit(solution)/shard_map/ppermute | solution.py:17
  7.6 32.1 %collective-permute-start.1 = (bf16[64,768]{0,1:T(8,128)(2,1)}, bf16[64,768]{0,1:T(8,128)(2,1)}, u32[]{:S(2)}, u32[]{:S(2)}) collective-permute-start(bf16[64,768]{0,1:T(8,128)(2,1)} %get-tuple-element.62), channel_id=1, source_target_pairs={{3,2},{7,6},{11,10},{15,14},{19,18},{23,22},{27,26},{31,30}} | collective-permute-start | bytes 294920 | tf_op jit(solution)/shard_map/ppermute | solution.py:38
  8.9 32.1 %collective-permute-start.2 = (bf16[64,768]{0,1:T(8,128)(2,1)}, bf16[64,768]{0,1:T(8,128)(2,1)}, u32[]{:S(2)}, u32[]{:S(2)}) collective-permute-start(bf16[64,768]{0,1:T(8,128)(2,1)} %get-tuple-element.61), channel_id=1, source_target_pairs={{3,1},{7,5},{11,9},{15,13},{19,17},{23,21},{27,25},{31,29}} | collective-permute-start | bytes 294920 | tf_op jit(solution)/shard_map/ppermute | solution.py:38
  11.1 27.2 %collective-permute-start = (bf16[192,768]{0,1:T(8,128)(2,1)}, bf16[192,768]{0,1:T(8,128)(2,1)S(1)}, u32[]{:S(2)}, u32[]{:S(2)}) collective-permute-start(bf16[192,768]{0,1:T(8,128)(2,1)} %slice_select_fusion.1), channel_id=1, source_target_pairs={{0,1},{1,2},{2,3},{3,0},{4,5},{5,6},{6,7},{7,4},{8,9},{9,10},{10,1... | collective-permute-start | bytes 884744 | tf_op jit(solution)/shard_map/ppermute | solution.py:31
  11.7 26.5 %all-to-all-start = ((bf16[4,2,192]{2,1,0:T(2,128)(2,1)}), bf16[4,2,192]{2,1,0:T(2,128)(2,1)S(1)}, u32[]{:S(2)}, u32[]{:S(2)}) async-start(bf16[4,2,192]{2,1,0:T(2,128)(2,1)} %tile.2), calls=%async_computation | async-start | bytes 8192 | tf_op jit(solution)/shard_map/all_to_all | solution.py:168
  38.3 11.1 %collective-permute-start.10 = (bf16[64,896]{0,1:T(8,128)(2,1)}, bf16[64,896]{0,1:T(8,128)(2,1)S(1)}, u32[]{:S(2)}, u32[]{:S(2)}) collective-permute-start(bf16[64,896]{0,1:T(8,128)(2,1)} %get-tuple-element.60), channel_id=1, source_target_pairs={{3,2},{7,6},{11,10},{15,14},{19,18},{23,22},{27,26},{31,30}} | collective-permute-start | bytes 344072 | tf_op jit(solution)/shard_map/ppermute | solution.py:38
  39.7 9.7 %collective-permute-start.11 = (bf16[64,896]{0,1:T(8,128)(2,1)S(1)}, bf16[64,896]{0,1:T(8,128)(2,1)S(1)}, u32[]{:S(2)}, u32[]{:S(2)}) collective-permute-start(bf16[64,896]{0,1:T(8,128)(2,1)S(1)} %copy-done.100), channel_id=1, source_target_pairs={{3,1},{7,5},{11,9},{15,13},{19,17},{23,21},{27,25},{31,29}} | collective-permute-start | bytes 344072 | tf_op jit(solution)/shard_map/ppermute | solution.py:38
  61.3 8.7 %collective-permute-start.5 = (bf16[768,768]{1,0:T(8,128)(2,1)}, bf16[768,768]{1,0:T(8,128)(2,1)S(1)}, u32[]{:S(2)}, u32[]{:S(2)}) collective-permute-start(bf16[768,768]{1,0:T(8,128)(2,1)} %collective-permute-done.4), channel_id=1, source_target_pairs={{0,1},{1,0},{2,3},{3,2},{4,5},{5,4},{6,7},{7,6},{8,9},{9,8},{10,11... | collective-permute-start | bytes 3538952 | tf_op jit(solution)/shard_map/ppermute | solution.py:17
  206.2 102.1 %collective-permute-start.14 = (bf16[64,768]{0,1:T(8,128)(2,1)}, bf16[64,768]{0,1:T(8,128)(2,1)}, u32[]{:S(2)}, u32[]{:S(2)}) collective-permute-start(bf16[64,768]{0,1:T(8,128)(2,1)} %slice.716), channel_id=1, source_target_pairs={{2,3},{6,7},{10,11},{14,15},{18,19},{22,23},{26,27},{30,31}} | collective-permute-start | bytes 294920 | tf_op jit(solution)/shard_map/ppermute | solution.py:56
  210.9 92.4 %collective-permute-start.16 = (bf16[768,768]{1,0:T(8,128)(2,1)}, bf16[768,768]{1,0:T(8,128)(2,1)}, u32[]{:S(2)}, u32[]{:S(2)}) collective-permute-start(bf16[768,768]{1,0:T(8,128)(2,1)} %pad_maximum_fusion.2), channel_id=1, source_target_pairs={{0,1},{1,0},{2,3},{3,2},{4,5},{5,4},{6,7},{7,6},{8,9},{9,8},{10,11... | collective-permute-start | bytes 3538952 | tf_op jit(solution)/shard_map/ppermute | solution.py:17
  211.7 74.6 %collective-permute-start.25 = (f32[2,192]{1,0:T(2,128)}, f32[2,192]{1,0:T(2,128)}, u32[]{:S(2)}, u32[]{:S(2)}) collective-permute-start(f32[2,192]{1,0:T(2,128)} %pad_maximum_fusion.40), channel_id=1, source_target_pairs={{0,1},{1,0},{2,3},{3,2},{4,5},{5,4},{6,7},{7,6},{8,9},{9,8},{10,11... | collective-permute-start | bytes 4616 | tf_op jit(solution)/shard_map/ppermute | solution.py:17
  212.9 74.7 %collective-permute-start.24 = (f32[2,192]{1,0:T(2,128)}, f32[2,192]{1,0:T(2,128)}, u32[]{:S(2)}, u32[]{:S(2)}) collective-permute-start(f32[2,192]{1,0:T(2,128)} %pad_maximum_fusion.39), channel_id=1, source_target_pairs={{0,1},{1,0},{2,3},{3,2},{4,5},{5,4},{6,7},{7,6},{8,9},{9,8},{10,11... | collective-permute-start | bytes 4616 | tf_op jit(solution)/shard_map/ppermute | solution.py:17
  225.9 66.0 %collective-permute-start.30 = (f32[8576]{0:T(1024)}, f32[8576]{0:T(1024)}, u32[]{:S(2)}, u32[]{:S(2)}) collective-permute-start(f32[8576]{0:T(1024)} %constant_dynamic-update-slice_fusion), channel_id=1, source_target_pairs={{0,1},{1,0},{2,3},{3,2},{4,5},{5,4},{6,7},{7,6},{8,9},{9,8},{10,11... | collective-permute-start | bytes 102920 | tf_op jit(solution)/shard_map/ppermute | solution.py:17
  287.7 76.5 %collective-permute-start.35 = (bf16[2,2,2,2,96,768]{5,4,0,1,2,3:T(8,128)(2,1)}, bf16[2,2,2,2,96,768]{5,4,0,1,2,3:T(8,128)(2,1)}, u32[]{:S(2)}, u32[]{:S(2)}) collective-permute-start(bf16[2,2,2,2,96,768]{5,4,0,1,2,3:T(8,128)(2,1)} %fusion.16), channel_id=1, source_target_pairs={{0,1},{1,0},{2,3},{3,2},{4,5},{5,4},{6,7},{7,6},{8,9},{9,8},{10,11... | collective-permute-start | bytes 7077896 | tf_op jit(solution)/shard_map/ppermute | solution.py:17
  297.7 64.3 %collective-permute-start.15 = (bf16[768,768]{1,0:T(8,128)(2,1)}, bf16[768,768]{1,0:T(8,128)(2,1)S(1)}, u32[]{:S(2)}, u32[]{:S(2)}) collective-permute-start(bf16[768,768]{1,0:T(8,128)(2,1)} %pad_maximum_fusion.1), channel_id=1, source_target_pairs={{0,1},{1,0},{2,3},{3,2},{4,5},{5,4},{6,7},{7,6},{8,9},{9,8},{10,11... | collective-permute-start | bytes 3538952 | tf_op jit(solution)/shard_map/ppermute | solution.py:17
  303.3 7.6 %collective-permute-start.33 = (f32[8576]{0:T(1024)S(1)}, f32[8576]{0:T(1024)S(1)}, u32[]{:S(2)}, u32[]{:S(2)}) collective-permute-start(f32[8576]{0:T(1024)S(1)} %add.586), channel_id=1, source_target_pairs={{0,8},{4,12},{8,0},{12,4},{16,24},{20,28},{24,16},{28,20},{1,9},{5... | collective-permute-start | bytes 102920 | tf_op jit(solution)/shard_map/ppermute | solution.py:17
  307.4 54.6 %collective-permute-start.17 = (bf16[768,768]{1,0:T(8,128)(2,1)}, bf16[768,768]{1,0:T(8,128)(2,1)}, u32[]{:S(2)}, u32[]{:S(2)}) collective-permute-start(bf16[768,768]{1,0:T(8,128)(2,1)} %fusion.21), channel_id=1, source_target_pairs={{0,2},{1,3},{2,0},{3,1},{4,6},{5,7},{6,4},{7,5},{8,10},{9,11},{10,... | collective-permute-start | bytes 3538952 | tf_op jit(solution)/shard_map/ppermute | solution.py:17
  308.3 28.2 %collective-permute-start.13 = (bf16[64,768]{0,1:T(8,128)(2,1)}, bf16[64,768]{0,1:T(8,128)(2,1)S(1)}, u32[]{:S(2)}, u32[]{:S(2)}) collective-permute-start(bf16[64,768]{0,1:T(8,128)(2,1)} %slice.716), channel_id=1, source_target_pairs={{1,3},{5,7},{9,11},{13,15},{17,19},{21,23},{25,27},{29,31}} | collective-permute-start | bytes 294920 | tf_op jit(solution)/shard_map/ppermute | solution.py:56
  310.9 32.6 %collective-permute-start.12 = (bf16[192,768]{0,1:T(8,128)(2,1)S(1)}, bf16[192,768]{0,1:T(8,128)(2,1)S(1)}, u32[]{:S(2)}, u32[]{:S(2)}) collective-permute-start(bf16[192,768]{0,1:T(8,128)(2,1)S(1)} %copy-done.99), channel_id=1, source_target_pairs={{1,0},{2,1},{3,2},{0,3},{5,4},{6,5},{7,6},{4,7},{9,8},{10,9},{11,1... | collective-permute-start | bytes 884744 | tf_op jit(solution)/shard_map/ppermute | solution.py:53
  343.6 9.9 %collective-permute-start.6 = (bf16[192,896]{0,1:T(8,128)(2,1)S(1)}, bf16[192,896]{0,1:T(8,128)(2,1)S(1)}, u32[]{:S(2)}, u32[]{:S(2)}) collective-permute-start(bf16[192,896]{0,1:T(8,128)(2,1)S(1)} %fusion.171), channel_id=1, source_target_pairs={{1,0},{2,1},{3,2},{0,3},{5,4},{6,5},{7,6},{4,7},{9,8},{10,9},{11,1... | collective-permute-start | bytes 1032200 | tf_op jit(solution)/shard_map/ppermute | solution.py:53
  343.6 36.1 %collective-permute-start.40 = (bf16[2,2,2,2,96,768]{5,4,0,1,2,3:T(8,128)(2,1)}, bf16[2,2,2,2,96,768]{5,4,0,1,2,3:T(8,128)(2,1)}, u32[]{:S(2)}, u32[]{:S(2)}) collective-permute-start(bf16[2,2,2,2,96,768]{5,4,0,1,2,3:T(8,128)(2,1)} %fusion.17), channel_id=1, source_target_pairs={{0,1},{1,0},{2,3},{3,2},{4,5},{5,4},{6,7},{7,6},{8,9},{9,8},{10,11... | collective-permute-start | bytes 7077896 | tf_op jit(solution)/shard_map/ppermute | solution.py:17
  363.9 15.6 %collective-permute-start.18 = (bf16[384,768]{1,0:T(8,128)(2,1)S(1)}, bf16[384,768]{1,0:T(8,128)(2,1)S(1)}, u32[]{:S(2)}, u32[]{:S(2)}) collective-permute-start(bf16[384,768]{1,0:T(8,128)(2,1)S(1)} %dynamic-slice_convert_fusion), channel_id=1, source_target_pairs={{0,4},{4,0},{8,12},{12,8},{16,20},{20,16},{24,28},{28,24},{1,5},{5... | collective-permute-start | bytes 1769480 | tf_op jit(solution)/shard_map/ppermute | solution.py:17
  368.1 34.1 %collective-permute-start.36 = (bf16[2,2,2,96,768]{4,3,0,1,2:T(8,128)(2,1)S(1)}, bf16[2,2,2,96,768]{4,3,0,1,2:T(8,128)(2,1)}, u32[]{:S(2)}, u32[]{:S(2)}) collective-permute-start(bf16[2,2,2,96,768]{4,3,0,1,2:T(8,128)(2,1)S(1)} %fusion.50), channel_id=1, source_target_pairs={{0,4},{4,0},{8,12},{12,8},{16,20},{20,16},{24,28},{28,24},{1,5},{5... | collective-permute-start | bytes 3538952 | tf_op jit(solution)/shard_map/ppermute | solution.py:17
  385.7 9.5 %collective-permute-start.20 = (bf16[96,768]{1,0:T(8,128)(2,1)S(1)}, bf16[96,768]{1,0:T(8,128)(2,1)S(1)}, u32[]{:S(2)}, u32[]{:S(2)}) collective-permute-start(bf16[96,768]{1,0:T(8,128)(2,1)S(1)} %dynamic-slice_convert_fusion.2), channel_id=1, source_target_pairs={{0,16},{4,20},{8,24},{12,28},{16,0},{20,4},{24,8},{28,12},{1,17},{... | collective-permute-start | bytes 442376 | tf_op jit(solution)/shard_map/ppermute | solution.py:17
  385.9 29.6 %collective-permute-start.41 = (bf16[2,2,2,96,768]{4,3,0,1,2:T(8,128)(2,1)S(1)}, bf16[2,2,2,96,768]{4,3,0,1,2:T(8,128)(2,1)}, u32[]{:S(2)}, u32[]{:S(2)}) collective-permute-start(bf16[2,2,2,96,768]{4,3,0,1,2:T(8,128)(2,1)S(1)} %fusion.51), channel_id=1, source_target_pairs={{0,2},{1,3},{2,0},{3,1},{4,6},{5,7},{6,4},{7,5},{8,10},{9,11},{10,... | collective-permute-start | bytes 3538952 | tf_op jit(solution)/shard_map/ppermute | solution.py:17
  401.4 16.1 %collective-permute-start.22 = (bf16[192,768]{1,0:T(8,128)(2,1)S(1)}, bf16[192,768]{1,0:T(8,128)(2,1)S(1)}, u32[]{:S(2)}, u32[]{:S(2)}) collective-permute-start(bf16[192,768]{1,0:T(8,128)(2,1)S(1)} %maximum_select_fusion.2), channel_id=1, source_target_pairs={{0,8},{4,12},{8,0},{12,4},{16,24},{20,28},{24,16},{28,20},{1,9},{5... | collective-permute-start | bytes 884744 | tf_op jit(solution)/shard_map/ppermute | solution.py:17
  404.7 18.7 %collective-permute-start.37 = (bf16[2,2,96,768]{3,2,0,1:T(8,128)(2,1)S(1)}, bf16[2,2,96,768]{3,2,0,1:T(8,128)(2,1)S(1)}, u32[]{:S(2)}, u32[]{:S(2)}) collective-permute-start(bf16[2,2,96,768]{3,2,0,1:T(8,128)(2,1)S(1)} %fusion.149), channel_id=1, source_target_pairs={{0,2},{1,3},{2,0},{3,1},{4,6},{5,7},{6,4},{7,5},{8,10},{9,11},{10,... | collective-permute-start | bytes 1769480 | tf_op jit(solution)/shard_map/ppermute | solution.py:17
  417.2 12.7 %collective-permute-start.42 = (bf16[2,2,96,768]{3,2,0,1:T(8,128)(2,1)S(1)}, bf16[2,2,96,768]{3,2,0,1:T(8,128)(2,1)S(1)}, u32[]{:S(2)}, u32[]{:S(2)}) collective-permute-start(bf16[2,2,96,768]{3,2,0,1:T(8,128)(2,1)S(1)} %fusion.150), channel_id=1, source_target_pairs={{0,4},{4,0},{8,12},{12,8},{16,20},{20,16},{24,28},{28,24},{1,5},{5... | collective-permute-start | bytes 1769480 | tf_op jit(solution)/shard_map/ppermute | solution.py:17
  417.7 18.5 %collective-permute-start.23 = (bf16[384,768]{1,0:T(8,128)(2,1)S(1)}, bf16[384,768]{1,0:T(8,128)(2,1)S(1)}, u32[]{:S(2)}, u32[]{:S(2)}) collective-permute-start(bf16[384,768]{1,0:T(8,128)(2,1)S(1)} %maximum_select_fusion.1), channel_id=1, source_target_pairs={{0,4},{4,0},{8,12},{12,8},{16,20},{20,16},{24,28},{28,24},{1,5},{5... | collective-permute-start | bytes 1769480 | tf_op jit(solution)/shard_map/ppermute | solution.py:17
  423.5 8.0 %collective-permute-start.38 = (bf16[2,96,768]{2,1,0:T(8,128)(2,1)S(1)}, bf16[2,96,768]{2,1,0:T(8,128)(2,1)S(1)}, u32[]{:S(2)}, u32[]{:S(2)}) collective-permute-start(bf16[2,96,768]{2,1,0:T(8,128)(2,1)S(1)} %fusion.182), channel_id=1, source_target_pairs={{0,8},{4,12},{8,0},{12,4},{16,24},{20,28},{24,16},{28,20},{1,9},{5... | collective-permute-start | bytes 884744 | tf_op jit(solution)/shard_map/ppermute | solution.py:17
  430.1 11.2 %collective-permute-start.43 = (bf16[2,96,768]{2,1,0:T(8,128)(2,1)S(1)}, bf16[2,96,768]{2,1,0:T(8,128)(2,1)S(1)}, u32[]{:S(2)}, u32[]{:S(2)}) collective-permute-start(bf16[2,96,768]{2,1,0:T(8,128)(2,1)S(1)} %fusion.183), channel_id=1, source_target_pairs={{0,8},{4,12},{8,0},{12,4},{16,24},{20,28},{24,16},{28,20},{1,9},{5... | collective-permute-start | bytes 884744 | tf_op jit(solution)/shard_map/ppermute | solution.py:17
  (203 other events, 1162.5 us)
